TPU v7x, 128 devices: a whole 4x4x4 slice. The times are simulated.
128 devices in a mesh: seq: 2 (over x_lo), ctx: 16 (over x_hi, z, core), fsdp: 4 (over y).
Axes of the slice: x: 4 (x_hi: 2, x_lo: 2; x = x_hi * 2 + x_lo), y: 4, z: 4, core: 2. Of those that a mesh axis runs over, the one named last changes fastest.
Arguments:
- tokens: bfloat16 [8, 2048, 960], P(('seq', 'fsdp'), 'ctx'), may hold values from -6 to 6
- gain_attn: bfloat16 [960], P('fsdp'), may hold values from 0.099609375 to 1.8984375
- w_q: bfloat16 [960, 960], P('fsdp'), may hold values from -0.375 to 0.375
- w_kv: bfloat16 [960, 640], P('fsdp'), may hold values from -0.1875 to 0.1875
- w_o: bfloat16 [960, 960], P('fsdp'), may hold values from -0.75 to 0.75
- gain_mlp: bfloat16 [960], P('fsdp'), may hold values from 0.099609375 to 1.8984375
- w_gate_up: bfloat16 [960, 5120], P('fsdp'), may hold values from -0.1875 to 0.1875
- w_down: bfloat16 [2560, 960], P('fsdp'), may hold values from -0.125 to 0.125
- block_order: int32 [8, 32], P(('seq', 'fsdp')), may hold values from 0 to 31, as said below
- cotangent: bfloat16 [8, 2048, 960], P(('seq', 'fsdp'), 'ctx'), may hold values from -6 to 6
Outputs:
- activations: bfloat16 [8, 2048, 960], P(('seq', 'fsdp'), 'ctx')
- input_grad: float32 [8, 2048, 960], P(('seq', 'fsdp'), 'ctx')
- grad_gain_attn: float32 [960], P('fsdp')
- grad_w_q: float32 [960, 960], P('fsdp')
- grad_w_kv: float32 [960, 640], P('fsdp')
- grad_w_o: float32 [960, 960], P('fsdp')
- grad_gain_mlp: float32 [960], P('fsdp')
- grad_w_gate_up: float32 [960, 5120], P('fsdp')
- grad_w_down: float32 [2560, 960], P('fsdp')
Inputs may be any that keep to these rules, and one draw needn't show every extreme that they name: `block_order`: each row is an order of the 32 causal blocks of its sequence; stored blocks 2 i and 2 i + 1 are causal blocks c and 31 - c for some c.
All inputs are finite; a program needn't handle non-finite values.
Results may differ from a plain program's by a relative error of at most 0.03.
Values may be sent and summed in bfloat16 or wider, within the bound.
No kernel may reach another device: no remote copies, remote signals or barrier semaphores. Data moves between devices by JAX's collectives and lax.ppermute only.
A program may use at most 128 MiB of HBM per device.

v0:
```python
import math

import jax
import jax.numpy as jnp
from jax import lax
from jax.sharding import PartitionSpec as P

HEADS = 15
KV_HEADS = 5
HEAD = 64
FF = 2560


EPS = 1e-05
THETA = 100000.0
FLOAT = jnp.float32
BHALF = jnp.bfloat16


def inner(left, right):
    return lax.dot_general(left, right, (((0,), (0,)), ((), ())), preferred_element_type=FLOAT)


def against(left, weight):
    return lax.dot_general(left, weight, (((1,), (1,)), ((), ())), preferred_element_type=FLOAT)


def tables(places):
    half = HEAD // 2
    freq = THETA ** (-(jnp.arange(half, dtype=FLOAT) * 2.0 / HEAD))
    angle = places.astype(FLOAT)[:, None] * freq[None, :]
    return (jnp.cos(angle)[:, None, :], jnp.sin(angle)[:, None, :])


def rotate(value, cosine, sine):
    half = HEAD // 2
    first, second = (value[..., :half], value[..., half:])
    return jnp.concatenate(
        [first * cosine - second * sine, second * cosine + first * sine], axis=-1
    )


def unrotate(grad, cosine, sine):
    half = HEAD // 2
    first, second = (grad[..., :half], grad[..., half:])
    return jnp.concatenate(
        [first * cosine + second * sine, second * cosine - first * sine], axis=-1
    )


def arrange(stored, index):
    blocks = index.shape[0]
    shaped = stored.reshape((blocks, stored.shape[0] // blocks) + stored.shape[1:])
    return jnp.take(shaped, index, axis=0).reshape(stored.shape)


def block_scores(query_block, key_block, start, key_span, query_places):
    scores = jnp.einsum(
        "tjge,kje->jgtk", query_block, key_block, preferred_element_type=FLOAT
    ) * HEAD ** (-0.5)
    allowed = (start + jnp.arange(key_span, dtype=jnp.int32))[None, :] <= query_places[:, None]
    return (scores, allowed)


def attend_forward(query_block, query_places, keys_sorted, values_sorted, key_span, block_count):
    stat_shape = (query_block.shape[1], query_block.shape[2], query_block.shape[0])

    def statistics(step_index, carry):
        running_max, running_sum = carry
        start = step_index * key_span
        key_block = lax.dynamic_slice_in_dim(keys_sorted, start, key_span, 0)
        scores, allowed = block_scores(query_block, key_block, start, key_span, query_places)
        new_max = jnp.maximum(running_max, jnp.max(jnp.where(allowed, scores, -1e30), axis=-1))
        fresh = jnp.sum(jnp.where(allowed, jnp.exp(scores - new_max[..., None]), 0.0), axis=-1)
        return (new_max, running_sum * jnp.exp(running_max - new_max) + fresh)

    running_max, running_sum = lax.fori_loop(
        0,
        block_count,
        statistics,
        (jnp.full(stat_shape, -jnp.inf, FLOAT), jnp.zeros(stat_shape, FLOAT)),
    )

    def weigh(step_index, accum):
        start = step_index * key_span
        key_block = lax.dynamic_slice_in_dim(keys_sorted, start, key_span, 0)
        value_block = lax.dynamic_slice_in_dim(values_sorted, start, key_span, 0)
        scores, allowed = block_scores(query_block, key_block, start, key_span, query_places)
        probs = (
            jnp.where(allowed, jnp.exp(scores - running_max[..., None]), 0.0)
            / running_sum[..., None]
        ).astype(BHALF)
        return accum + jnp.einsum(
            "jgtk,kje->tjge", probs, value_block, preferred_element_type=FLOAT
        )

    weighted = lax.fori_loop(0, block_count, weigh, jnp.zeros(query_block.shape, FLOAT))
    return (weighted, running_max, running_sum)


def attend_backward(
    query_block,
    query_places,
    keys_sorted,
    values_sorted,
    running_max,
    running_sum,
    grad_block,
    delta,
    key_span,
    block_count,
    carried,
):
    scale = HEAD ** (-0.5)

    def accumulate(step_index, carry):
        query_grad, key_grad, value_grad = carry
        start = step_index * key_span
        key_block = lax.dynamic_slice_in_dim(keys_sorted, start, key_span, 0)
        value_block = lax.dynamic_slice_in_dim(values_sorted, start, key_span, 0)
        scores, allowed = block_scores(query_block, key_block, start, key_span, query_places)
        probs = (
            jnp.where(allowed, jnp.exp(scores - running_max[..., None]), 0.0)
            / running_sum[..., None]
        )
        prob_grad = jnp.einsum(
            "tjge,kje->jgtk", grad_block, value_block, preferred_element_type=FLOAT
        )
        score_grad = (probs * (prob_grad - delta[..., None])).astype(BHALF)
        query_grad = (
            query_grad
            + jnp.einsum("jgtk,kje->tjge", score_grad, key_block, preferred_element_type=FLOAT)
            * scale
        )
        key_part = (
            jnp.einsum("jgtk,tjge->kje", score_grad, query_block, preferred_element_type=FLOAT)
            * scale
        )
        value_part = jnp.einsum(
            "jgtk,tjge->kje", probs.astype(BHALF), grad_block, preferred_element_type=FLOAT
        )
        key_grad = lax.dynamic_update_slice_in_dim(
            key_grad, lax.dynamic_slice_in_dim(key_grad, start, key_span, 0) + key_part, start, 0
        )
        value_grad = lax.dynamic_update_slice_in_dim(
            value_grad,
            lax.dynamic_slice_in_dim(value_grad, start, key_span, 0) + value_part,
            start,
            0,
        )
        return (query_grad, key_grad, value_grad)

    start_carry = (jnp.zeros(query_block.shape, FLOAT), carried[0], carried[1])
    return lax.fori_loop(0, block_count, accumulate, start_carry)


def shards(tokens, gain_attn, w_q, w_kv, w_o, gain_mlp, w_gate_up, w_down, block_order, cotangent):
    width = HEADS * HEAD
    kv_width = KV_HEADS * HEAD
    group = HEADS // KV_HEADS
    inputs = tokens[0].astype(FLOAT)
    rows = inputs.shape[0]
    blk_rows = rows // 2
    order = block_order[0]
    blocks = order.shape[0]
    seq_len = blocks * blk_rows
    key_span = math.gcd(seq_len, 256)
    place = lax.axis_index("ctx")
    mine = lax.dynamic_slice_in_dim(order, place * 2, 2)
    own_places = (
        mine[:, None] * blk_rows + jnp.arange(blk_rows, dtype=jnp.int32)[None, :]
    ).reshape(rows)
    slots = jnp.arange(blocks, dtype=jnp.int32)
    inverse = jnp.sum(jnp.where(order[None, :] == slots[:, None], slots[None, :], 0), axis=1)
    gain_one, weight_q, weight_kv, weight_o, gain_two, weight_gu, weight_down = (
        lax.all_gather(gain_attn, "fsdp", axis=0, tiled=True),
        lax.all_gather(w_q, "fsdp", axis=0, tiled=True),
        lax.all_gather(w_kv, "fsdp", axis=0, tiled=True),
        lax.all_gather(w_o, "fsdp", axis=0, tiled=True),
        lax.all_gather(gain_mlp, "fsdp", axis=0, tiled=True),
        lax.all_gather(w_gate_up, "fsdp", axis=0, tiled=True),
        lax.all_gather(w_down, "fsdp", axis=0, tiled=True),
    )
    inv_one = lax.rsqrt(jnp.mean(inputs * inputs, axis=-1, keepdims=True) + EPS)
    normed = (inputs * inv_one * gain_one.astype(FLOAT)).astype(BHALF)
    cosine, sine = tables(own_places)
    query_lin = jnp.dot(normed, weight_q, preferred_element_type=FLOAT).reshape(rows, HEADS, HEAD)
    queries = rotate(query_lin, cosine, sine).astype(BHALF).reshape(rows, KV_HEADS, group, HEAD)
    kv_lin = jnp.dot(normed, weight_kv, preferred_element_type=FLOAT)
    key_own = (
        rotate(kv_lin[:, :kv_width].reshape(rows, KV_HEADS, HEAD), cosine, sine)
        .astype(BHALF)
        .reshape(rows, kv_width)
    )
    value_own = kv_lin[:, kv_width:].astype(BHALF)
    keys_all, values_all = (
        lax.all_gather(key_own, "ctx", axis=0, tiled=True),
        lax.all_gather(value_own, "ctx", axis=0, tiled=True),
    )
    keys_sorted = arrange(keys_all, inverse).reshape(seq_len, KV_HEADS, HEAD)
    values_sorted = arrange(values_all, inverse).reshape(seq_len, KV_HEADS, HEAD)
    counts = [
        ((mine[half_index] + 1) * blk_rows + key_span - 1) // key_span for half_index in range(2)
    ]
    pieces = []
    maxima = []
    totals = []
    for half_index in range(2):
        query_block = queries[half_index * blk_rows : (half_index + 1) * blk_rows]
        query_places = own_places[half_index * blk_rows : (half_index + 1) * blk_rows]
        weighted, running_max, running_sum = attend_forward(
            query_block, query_places, keys_sorted, values_sorted, key_span, counts[half_index]
        )
        pieces.append(weighted)
        maxima.append(running_max)
        totals.append(running_sum)
    attended = jnp.concatenate(pieces, axis=0)
    mixed = attended.reshape(rows, width).astype(BHALF)
    resid = inputs + jnp.dot(mixed, weight_o, preferred_element_type=FLOAT)
    inv_two = lax.rsqrt(jnp.mean(resid * resid, axis=-1, keepdims=True) + EPS)
    normed_two = (resid * inv_two * gain_two.astype(FLOAT)).astype(BHALF)
    gate_up = jnp.dot(normed_two, weight_gu, preferred_element_type=FLOAT)
    gate = gate_up[:, :FF]
    up_part = gate_up[:, FF:]
    sigmoid_gate = jax.nn.sigmoid(gate)
    activated = gate * sigmoid_gate
    hidden = (activated * up_part).astype(BHALF)
    result = resid + jnp.dot(hidden, weight_down, preferred_element_type=FLOAT)
    gain_one, weight_q, weight_kv, weight_o, gain_two, weight_gu, weight_down = (
        lax.all_gather(gain_attn, "fsdp", axis=0, tiled=True),
        lax.all_gather(w_q, "fsdp", axis=0, tiled=True),
        lax.all_gather(w_kv, "fsdp", axis=0, tiled=True),
        lax.all_gather(w_o, "fsdp", axis=0, tiled=True),
        lax.all_gather(gain_mlp, "fsdp", axis=0, tiled=True),
        lax.all_gather(w_gate_up, "fsdp", axis=0, tiled=True),
        lax.all_gather(w_down, "fsdp", axis=0, tiled=True),
    )
    keys_back, values_back = (
        lax.all_gather(key_own, "ctx", axis=0, tiled=True),
        lax.all_gather(value_own, "ctx", axis=0, tiled=True),
    )
    keys_sorted = arrange(keys_back, inverse).reshape(seq_len, KV_HEADS, HEAD)
    values_sorted = arrange(values_back, inverse).reshape(seq_len, KV_HEADS, HEAD)
    out_grad = cotangent[0]
    out_float = out_grad.astype(FLOAT)
    grad_down = inner(hidden, out_grad)
    hidden_grad = against(out_grad, weight_down)
    gate_grad = hidden_grad * up_part * sigmoid_gate * (1.0 + gate * (1.0 - sigmoid_gate))
    up_grad = hidden_grad * activated
    gate_up_grad = jnp.concatenate([gate_grad, up_grad], axis=1).astype(BHALF)
    grad_gu = inner(normed_two, gate_up_grad)
    normed_two_grad = against(gate_up_grad, weight_gu)
    grad_gain_two = jnp.sum(normed_two_grad * resid * inv_two, axis=0)
    scaled_two = gain_two.astype(FLOAT) * normed_two_grad
    resid_grad = (
        out_float
        + inv_two * scaled_two
        - resid * inv_two * inv_two * inv_two * jnp.mean(scaled_two * resid, axis=-1, keepdims=True)
    )
    resid_low = resid_grad.astype(BHALF)
    grad_o = inner(mixed, resid_low)
    mixed_grad = against(resid_low, weight_o).astype(BHALF).reshape(rows, KV_HEADS, group, HEAD)
    delta_all = jnp.moveaxis(jnp.sum(mixed_grad.astype(FLOAT) * attended, axis=-1), 0, -1)
    carried = (
        jnp.zeros((seq_len, KV_HEADS, HEAD), FLOAT),
        jnp.zeros((seq_len, KV_HEADS, HEAD), FLOAT),
    )
    query_grads = []
    for half_index in range(2):
        lower = half_index * blk_rows
        upper = (half_index + 1) * blk_rows
        query_grad, key_grad, value_grad = attend_backward(
            queries[lower:upper],
            own_places[lower:upper],
            keys_sorted,
            values_sorted,
            maxima[half_index],
            totals[half_index],
            mixed_grad[lower:upper],
            delta_all[..., lower:upper],
            key_span,
            counts[half_index],
            carried,
        )
        carried = (key_grad, value_grad)
        query_grads.append(query_grad)
    key_stored = arrange(carried[0], order).reshape(seq_len, kv_width)
    value_stored = arrange(carried[1], order).reshape(seq_len, kv_width)
    kv_grad = lax.psum_scatter(
        jnp.concatenate([key_stored, value_stored], axis=1).astype(jnp.bfloat16),
        "ctx",
        scatter_dimension=0,
        tiled=True,
    ).astype(jnp.float32)
    key_lin_grad = unrotate(
        kv_grad[:, :kv_width].reshape(rows, KV_HEADS, HEAD), cosine, sine
    ).reshape(rows, kv_width)
    kv_low = jnp.concatenate([key_lin_grad, kv_grad[:, kv_width:]], axis=1).astype(BHALF)
    query_all = jnp.concatenate(query_grads, axis=0).reshape(rows, HEADS, HEAD)
    query_low = unrotate(query_all, cosine, sine).reshape(rows, width).astype(BHALF)
    grad_q = inner(normed, query_low)
    grad_kv = inner(normed, kv_low)
    normed_grad = against(query_low, weight_q) + against(kv_low, weight_kv)
    grad_gain_one = jnp.sum(normed_grad * inputs * inv_one, axis=0)
    scaled_one = gain_one.astype(FLOAT) * normed_grad
    input_grad = (
        resid_grad
        + inv_one * scaled_one
        - inputs
        * inv_one
        * inv_one
        * inv_one
        * jnp.mean(scaled_one * inputs, axis=-1, keepdims=True)
    )
    shard_grads = (
        lax.psum_scatter(
            grad_gain_one.astype(jnp.bfloat16), "fsdp", scatter_dimension=0, tiled=True
        ).astype(jnp.float32),
        lax.psum_scatter(
            grad_q.astype(jnp.bfloat16), "fsdp", scatter_dimension=0, tiled=True
        ).astype(jnp.float32),
        lax.psum_scatter(
            grad_kv.astype(jnp.bfloat16), "fsdp", scatter_dimension=0, tiled=True
        ).astype(jnp.float32),
        lax.psum_scatter(
            grad_o.astype(jnp.bfloat16), "fsdp", scatter_dimension=0, tiled=True
        ).astype(jnp.float32),
        lax.psum_scatter(
            grad_gain_two.astype(jnp.bfloat16), "fsdp", scatter_dimension=0, tiled=True
        ).astype(jnp.float32),
        lax.psum_scatter(
            grad_gu.astype(jnp.bfloat16), "fsdp", scatter_dimension=0, tiled=True
        ).astype(jnp.float32),
        lax.psum_scatter(
            grad_down.astype(jnp.bfloat16), "fsdp", scatter_dimension=0, tiled=True
        ).astype(jnp.float32),
    )
    total_grads = (
        lax.psum(shard_grads[0].astype(jnp.bfloat16), ("seq", "ctx")).astype(jnp.float32),
        lax.psum(shard_grads[1].astype(jnp.bfloat16), ("seq", "ctx")).astype(jnp.float32),
        lax.psum(shard_grads[2].astype(jnp.bfloat16), ("seq", "ctx")).astype(jnp.float32),
        lax.psum(shard_grads[3].astype(jnp.bfloat16), ("seq", "ctx")).astype(jnp.float32),
        lax.psum(shard_grads[4].astype(jnp.bfloat16), ("seq", "ctx")).astype(jnp.float32),
        lax.psum(shard_grads[5].astype(jnp.bfloat16), ("seq", "ctx")).astype(jnp.float32),
        lax.psum(shard_grads[6].astype(jnp.bfloat16), ("seq", "ctx")).astype(jnp.float32),
    )
    return (
        result.astype(BHALF)[None],
        input_grad[None],
        total_grads[0],
        total_grads[1],
        total_grads[2],
        total_grads[3],
        total_grads[4],
        total_grads[5],
        total_grads[6],
    )


def solution(mesh):
    placed = (
        P(("seq", "fsdp"), "ctx", None),
        P("fsdp"),
        P("fsdp", None),
        P("fsdp", None),
        P("fsdp", None),
        P("fsdp"),
        P("fsdp", None),
        P("fsdp", None),
        P(("seq", "fsdp"), None),
        P(("seq", "fsdp"), "ctx", None),
    )
    return jax.shard_map(
        shards,
        mesh=mesh,
        in_specs=placed,
        out_specs=(
            P(("seq", "fsdp"), "ctx", None),
            P(("seq", "fsdp"), "ctx", None),
            P("fsdp"),
            P("fsdp", None),
            P("fsdp", None),
            P("fsdp", None),
            P("fsdp"),
            P("fsdp", None),
            P("fsdp", None),
        ),
        check_vma=False,
    )
```

profile of v0, /device:TPU:1, one launch (start us, length us, event | category | flops | bytes accessed | tf_op | source)
XLA Modules:
  0.0 917.5 jit_solution(17884635963121614197)
XLA Ops:
  12.4 9.5 %all-reduce.7 = (bf16[960]{0:T(1024)(128)(2,1)S(1)}, bf16[960]{0:T(1024)(128)(2,1)S(1)}) all-reduce(bf16[960]{0:T(1024)(128)(2,1)S(1)} %dynamic-update-slice, bf16[960]{0:T(1024)(128)(2,1)S(1)} %dynamic-update-slice.1), channel_id=1, replica_groups=mesh['seq'=2,'ctx'=16,'fsdp'=4] {'fsdp'}, use_global_device_ids=true, to_apply=%add | all-reduce | flops 1920 | bytes 7680
  24.2 12.3 %all-gather.8.cloned.1.call-done = bf16[960,640]{1,0:T(8,128)(2,1)} async-done(((bf16[240,640]{1,0:T(8,128)(2,1)}), bf16[960,640]{1,0:T(8,128)(2,1)}) %all-gather.8.cloned.1.call-update) | async-done | bytes 1228816 | tf_op jit(solution)/shard_map/all_gather | solution.py:178
  44.3 25.3 %all-gather.14.cloned.1.call-done = bf16[960,960]{1,0:T(8,128)(2,1)} async-done(((bf16[240,960]{1,0:T(8,128)(2,1)}), bf16[960,960]{1,0:T(8,128)(2,1)}) %all-gather.14.cloned.1.call-update) | async-done | bytes 1843216 | tf_op jit(solution)/shard_map/all_gather | solution.py:177
  69.6 3.9 copy.91
  76.4 40.4 %all-gather.12.cloned.1.call-done = bf16[2048,320]{0,1:T(8,128)(2,1)} async-done(((bf16[128,320]{0,1:T(8,128)(2,1)}), bf16[2048,320]{0,1:T(8,128)(2,1)}) %all-gather.12.cloned.1.call-update) | async-done | bytes 1310736 | tf_op jit(solution)/shard_map/all_gather | solution.py:197
  119.3 3.3 gather_fusion.1
  122.6 42.9 %all-gather.10.cloned.1.call-done = bf16[2048,320]{1,0:T(8,128)(2,1)} async-done(((bf16[128,320]{1,0:T(8,128)(2,1)}), bf16[2048,320]{1,0:T(8,128)(2,1)}) %all-gather.10.cloned.1.call-update) | async-done | bytes 1310736 | tf_op jit(solution)/shard_map/all_gather | solution.py:198
  165.5 3.3 gather_fusion
  168.8 4.0 broadcast_select_fusion
  172.8 5.9 copy.87
  178.7 4.7 reshape_reshape.16
  183.4 5.9 copy.90
  189.3 3.9 reshape_reshape.17
  193.2 2.8 while.74
  196.1 4.9 while.75
  201.0 5.7 while.72
  207.6 15.8 %while.73 = (s32[]{:T(128)}, f32[64,5,3,64]{0,3,2,1:T(8,128)}, s32[]{:T(128)}, bf16[2048,5,64]{0,2,1:T(8,128)(2,1)}, s32[64]{0:T(128)S(1)}, /*index=5*/bf16[2048...) while((s32[]{:T(128)}, f32[64,5,3,64]{0,3,2,1:T(8,128)}, ...), condition=%wide.region_7.9_spmd, body=%wide.region_6.8_spmd.sunk | while | flops 64221444 | bytes 1367479 | solution.py:97
  227.5 64.5 %all-gather.18.cloned.1.call-done = bf16[960,5120]{1,0:T(8,128)(2,1)} async-done(((bf16[240,5120]{1,0:T(8,128)(2,1)}), bf16[960,5120]{1,0:T(8,128)(2,1)}) %all-gather.18.cloned.1.call-update) | async-done | bytes 9830416 | tf_op jit(solution)/shard_map/all_gather | solution.py:181
  292.0 7.0 fusion.145
  299.0 49.9 %all-gather.20.cloned.1.call-done = bf16[2560,960]{0,1:T(8,128)(2,1)} async-done(((bf16[640,960]{0,1:T(8,128)(2,1)}), bf16[2560,960]{0,1:T(8,128)(2,1)}) %all-gather.20.cloned.1.call-update) | async-done | bytes 4915216 | tf_op jit(solution)/shard_map/all_gather | solution.py:182
  348.9 5.5 multiply_convert_fusion.1
  355.1 3.4 multiply_reduce_fusion
  363.2 38.1 %while.76 = (s32[]{:T(128)}, f32[64,5,3,64]{0,3,2,1:T(8,128)}, f32[2048,5,64]{0,2,1:T(8,128)S(1)}, f32[2048,5,64]{0,2,1:T(8,128)}, s32[]{:T(128)}, /*index=5*/bf...) while((s32[]{:T(128)}, f32[64,5,3,64]{0,3,2,1:T(8,128)}, ...), condition=%wide.region_18.20_spmd, body=%wide.region_17.19_spmd.sunk | while | flops 159637760 | bytes 9344803 | solution.py:154
  401.4 19.5 %while.77 = (s32[]{:T(128)}, f32[64,5,3,64]{0,3,2,1:T(8,128)S(1)}, f32[2048,5,64]{0,2,1:T(8,128)S(1)}, f32[2048,5,64]{0,2,1:T(8,128)}, s32[]{:T(128)}, /*index=5...) while((s32[]{:T(128)}, f32[64,5,3,64]{0,3,2,1:T(8,128)S(1)}, ...), condition=%wide.region_20.22_spmd, body=%wide.region_19.21_spmd.sunk | while | flops 159637760 | bytes 7993095 | solution.py:154
  421.0 3.5 reshape.279
  424.5 4.8 copy.96
  429.3 3.5 reshape.280
  432.8 4.9 copy.98
  440.0 4.3 gather_fusion.3
  444.3 6.0 select_convert_fusion.1
  450.2 3.5 copy.99
  453.8 2.8 reshape_reshape.19
  456.6 3.5 copy.97
  460.1 2.8 reshape_reshape.18
  468.6 3.7 convolution_convert_fusion.1
  472.3 7.9 copy.120
  486.0 54.6 %reduce-scatter.19.cloned.1.call-done = bf16[128,640]{1,0:T(8,128)(2,1)} async-done(((bf16[2048,640]{1,0:T(8,128)(2,1)}), bf16[128,640]{1,0:T(8,128)(2,1)}) %reduce-scatter.19.cloned.1.call-update) | async-done | bytes 163856
  543.7 5.3 convolution_convert_fusion
  549.1 49.7 %reduce-scatter.21.cloned.1.call-done = bf16[640,960]{1,0:T(8,128)(2,1)} async-done(((bf16[2560,960]{1,0:T(8,128)(2,1)}), bf16[640,960]{1,0:T(8,128)(2,1)}) %reduce-scatter.21.cloned.1.call-update) | async-done | bytes 1228816
  601.2 28.8 %reduce-scatter.11.cloned.1.call-done = bf16[240,960]{1,0:T(8,128)(2,1)} async-done(((bf16[960,960]{1,0:T(8,128)(2,1)}), bf16[240,960]{1,0:T(8,128)(2,1)}) %reduce-scatter.11.cloned.1.call-update) | async-done | bytes 460816 | tf_op jit(solution)/shard_map/reduce_scatter | solution.py:319
  630.0 31.4 %reduce-scatter.15.cloned.1.call-done = bf16[240,960]{1,0:T(8,128)(2,1)} async-done(((bf16[960,960]{1,0:T(8,128)(2,1)}), bf16[240,960]{1,0:T(8,128)(2,1)}) %reduce-scatter.15.cloned.1.call-update) | async-done | bytes 460816 | tf_op jit(solution)/shard_map/reduce_scatter | solution.py:325
  661.4 25.1 %reduce-scatter.13.cloned.1.call-done = bf16[240,640]{1,0:T(8,128)(2,1)} async-done(((bf16[960,640]{1,0:T(8,128)(2,1)}), bf16[240,640]{1,0:T(8,128)(2,1)}) %reduce-scatter.13.cloned.1.call-update) | async-done | bytes 307216 | tf_op jit(solution)/shard_map/reduce_scatter | solution.py:322
  686.5 95.8 %reduce-scatter.17.cloned.1.call-done = bf16[240,5120]{1,0:T(8,128)(2,1)} async-done(((bf16[960,5120]{1,0:T(8,128)(2,1)}), bf16[240,5120]{1,0:T(8,128)(2,1)}) %reduce-scatter.17.cloned.1.call-update) | async-done | bytes 2457616 | tf_op jit(solution)/shard_map/reduce_scatter | solution.py:331
  785.0 4.6 fusion.106
  790.3 6.5 all-reduce.6
  796.9 65.0 %all-reduce.4 = (bf16[240]{0:T(256)(128)(2,1)S(1)}, bf16[240]{0:T(256)(128)(2,1)S(1)}) all-reduce(bf16[240]{0:T(256)(128)(2,1)S(1)} %dynamic-slice.4, bf16[240]{0:T(256)(128)(2,1)S(1)} %dynamic-slice.6), channel_id=1, replica_groups=mesh['seq'=2,'ctx'=16,'fsdp'=4] {'seq','ctx'}, use_global_device_ids=true, to_apply=%region_25.28 | all-reduce | flops 480 | bytes 1920 | tf_op jit(solution)/shard_map/psum | solution.py:339
  864.1 35.9 %all-reduce.10.cloned.1.call-done = (bf16[240,960]{1,0:T(8,128)(2,1)}, bf16[240,640]{1,0:T(8,128)(2,1)}, bf16[240,960]{1,0:T(8,128)(2,1)}, bf16[240,5120]{1,0:T(8,128)(2,1)}, bf16[640,960]{0,1:T(8,128)(2,1)}) async-done(((bf16[240,960]{1,0:T(8,128)(2,1)}, bf16[240,640]{1,0:T(8,128)(2,1)}, bf16[240,960]{1,0:T(8,128)(2,1)}, bf16[240,5120]{1,0:T(8,128)(2,1)}, bf16[640,960]{0,1:T(8,128)(2,1)}), ...) | async-done | bytes 4915216 | tf_op jit(solution)/shard_map/psum | solution.py:340
  906.1 2.8 convert_element_type.199
  (364 shorter events, 145.6 us)
Async XLA Ops:
  7.2 29.3 %all-gather.8.cloned.1.call-start = ((), (), s32[]{:S(2)}) async-start(), calls=%async_computation.6 | async-start | bytes 1536000 | tf_op jit(solution)/shard_map/all_gather | solution.py:178
  7.9 61.7 %all-gather.14.cloned.1.call-start = ((), (), s32[]{:S(2)}) async-start(), calls=%async_computation.9 | async-start | bytes 2457600 | tf_op jit(solution)/shard_map/all_gather | solution.py:177
  8.7 108.1 %all-gather.12.cloned.1.call-start = ((), (), s32[]{:S(2)}) async-start(), calls=%async_computation.8 | async-start | bytes 1392640 | tf_op jit(solution)/shard_map/all_gather | solution.py:197
  24.2 457.3 %copy-start.34 = (f32[128,32]{0,1:T(8,128)}, f32[128,32]{0,1:T(8,128)S(1)}, u32[]{:S(2)}) copy-start(f32[128,32]{0,1:T(8,128)S(1)} %get-tuple-element.656) | copy-start | bytes 49156
  39.3 126.2 %all-gather.10.cloned.1.call-start = ((), (), s32[]{:S(2)}) async-start(), calls=%async_computation.7 | async-start | bytes 1671168 | tf_op jit(solution)/shard_map/all_gather | solution.py:198
  40.1 184.8 %all-gather.16.cloned.1.call-start = ((), (), s32[]{:S(2)}) async-start(), calls=%async_computation.10 | async-start | bytes 2457600 | tf_op jit(solution)/shard_map/all_gather | solution.py:179
  40.7 2.6 copy-start.37
  40.7 251.3 %all-gather.18.cloned.1.call-start = ((), (), s32[]{:S(2)}) async-start(), calls=%async_computation.11 | async-start | bytes 12288000 | tf_op jit(solution)/shard_map/all_gather | solution.py:181
  41.3 307.6 %all-gather.20.cloned.1.call-start = ((), (), s32[]{:S(2)}) async-start(), calls=%async_computation.12 | async-start | bytes 6144000 | tf_op jit(solution)/shard_map/all_gather | solution.py:182
  42.0 498.5 %reduce-scatter.19.cloned.1.call-start = ((), (), s32[]{:S(2)}) async-start(), calls=%async_computation.17 | async-start | bytes 2785280
  69.6 3.9 copy-start.10
  76.0 46.6 %copy-start.12 = (bf16[64,15,64]{0,2,1:T(8,128)(2,1)}, bf16[64,15,64]{0,2,1:T(8,128)(2,1)S(1)}, u32[]{:S(2)}) copy-start(bf16[64,15,64]{0,2,1:T(8,128)(2,1)S(1)} %get-tuple-element.644) | copy-start | bytes 368644
  223.4 4.1 copy-start.7
  224.9 74.1 %copy-start.23 = (bf16[128,5,3,64]{0,3,2,1:T(8,128)(2,1)}, bf16[128,5,3,64]{0,3,2,1:T(8,128)(2,1)S(1)}, u32[]{:S(2)}) copy-start(bf16[128,5,3,64]{0,3,2,1:T(8,128)(2,1)S(1)} %fusion.132) | copy-start | bytes 737284
  227.4 131.1 %copy-start.8 = (f32[128,960]{0,1:T(8,128)}, f32[128,960]{0,1:T(8,128)S(1)}, u32[]{:S(2)}) copy-start(f32[128,960]{0,1:T(8,128)S(1)} %get-tuple-element.668) | copy-start | bytes 1474564
  292.0 56.9 %copy-start.25 = (bf16[1,128,960]{1,2,0:T(8,128)(2,1)S(1)}, bf16[1,128,960]{1,2,0:T(8,128)(2,1)}, u32[]{:S(2)}) copy-start(bf16[1,128,960]{1,2,0:T(8,128)(2,1)} %param.35) | copy-start | bytes 737284
  348.9 6.2 copy-start.6
  354.4 4.1 copy-start.30
  354.4 4.1 copy-start.32
  355.1 3.6 copy-start.15
  367.3 2.3 copy-start.2
  373.7 2.3 copy-start.2
  380.0 2.3 copy-start.2
  386.4 2.3 copy-start.2
  392.8 2.3 copy-start.2
  399.1 2.3 copy-start.2
  403.0 2.6 copy-start.13
  409.5 2.6 copy-start.13
  415.9 2.6 copy-start.13
  424.5 4.8 copy-start
  432.8 4.9 copy-start.4
  440.0 4.3 copy-start.5
  467.5 131.3 %reduce-scatter.21.cloned.1.call-start = ((), (), s32[]{:S(2)}) async-start(), calls=%async_computation.18 | async-start | bytes 6553600
  480.3 149.8 %reduce-scatter.11.cloned.1.call-start = ((), (), s32[]{:S(2)}) async-start(), calls=%async_computation.13 | async-start | bytes 2457600 | tf_op jit(solution)/shard_map/reduce_scatter | solution.py:319
  481.6 2.1 copy-start.17
  481.6 2.1 copy-start.24
  483.6 177.8 %reduce-scatter.15.cloned.1.call-start = ((), (), s32[]{:S(2)}) async-start(), calls=%async_computation.15 | async-start | bytes 2457600 | tf_op jit(solution)/shard_map/reduce_scatter | solution.py:325
  485.7 56.3 %copy-start.35 = (f32[128,32]{0,1:T(8,128)S(1)}, f32[128,32]{0,1:T(8,128)}, u32[]{:S(2)}) copy-start(f32[128,32]{0,1:T(8,128)} %copy-done.34) | copy-start | bytes 49156
  485.7 200.9 %reduce-scatter.13.cloned.1.call-start = ((), (), s32[]{:S(2)}) async-start(), calls=%async_computation.14 | async-start | bytes 1536000 | tf_op jit(solution)/shard_map/reduce_scatter | solution.py:322
  541.6 2.0 copy-start.9
  541.6 2.0 copy-start.31
  542.0 7.0 copy-start.28
  543.6 238.7 %reduce-scatter.17.cloned.1.call-start = ((), (), s32[]{:S(2)}) async-start(), calls=%async_computation.16 | async-start | bytes 12288000 | tf_op jit(solution)/shard_map/reduce_scatter | solution.py:331
  549.0 351.0 %all-reduce.10.cloned.1.call-start = ((), (), s32[]{:S(2)}) async-start(), calls=%async_computation.19 | async-start | bytes 9953280 | tf_op jit(solution)/shard_map/psum | solution.py:340
  785.0 4.6 copy-start.18
  785.0 4.6 copy-start.29
  900.0 6.1 copy-start.22
  906.1 2.8 copy-start.27
  (16 other events, 20.7 us)
Sparse Core Ops, SparseCore 0:
  9.7 26.7 all-gather.7
  38.1 31.3 all-gather.13
  72.4 44.3 all-gather.11
  119.7 45.7 all-gather.9
  167.0 28.1 all-gather.15
  196.7 95.2 all-gather.17
  293.7 55.1 all-gather.19
  467.6 72.8 reduce-scatter.18
  543.0 55.7 reduce-scatter.20
  601.6 28.3 reduce-scatter.10
  633.0 28.3 reduce-scatter.14
  663.7 22.8 reduce-scatter.12
  689.2 93.0 reduce-scatter.16
  786.3 113.6 all-reduce.9
where the time goes:
time: 928 us; the launch traced here: 918 us
  waiting for transfers between devices  560 us (60%)
  matrix products  123 us (13%)
  local copies, waits for them, and re-layouts  97.4 us (10%)
  blocking collectives  81.1 us (9%)
  other arithmetic  36 us (4%)
  between operations  17.8 us (2%)
    unnamed x16, waiting for transfers between devices  108 us
    reduce_scatter x1, waiting for transfers between devices, shards(): lax.psum_scatter(grad_gu.astype(jnp.bfloat16), 'fsdp', scatter_dimension=...  95.8 us
    psum x1, blocking collectives, shards(): lax.psum(shard_grads[0].astype(jnp.bfloat16), ('seq', 'ctx'))  65 us
    all_gather x1, waiting for transfers between devices, shards(): lax.all_gather(w_gate_up, 'fsdp', axis=0, tiled=True)  64.5 us
    all_gather x1, waiting for transfers between devices, shards(): lax.all_gather(w_down, 'fsdp', axis=0, tiled=True)  49.9 us
    all_gather x1, waiting for transfers between devices, shards(): lax.all_gather(value_own, 'ctx', axis=0, tiled=True)  42.9 us
    all_gather x1, waiting for transfers between devices, shards(): lax.all_gather(key_own, 'ctx', axis=0, tiled=True)  40.4 us
    psum x1, waiting for transfers between devices, shards(): lax.psum(shard_grads[1].astype(jnp.bfloat16), ('seq', 'ctx'))  35.9 us
  transfers between devices with their start and end apart: 14, of which 13 were waited for; matrix products, arithmetic and copies ran while one was open for 14% of the time, Pallas kernels for 0%

commit v1 on v0

v1 whole, which is shorter than its diff:
```python
import functools

import jax
import jax.numpy as jnp
from jax import lax
from jax.experimental import pallas as pl
from jax.experimental.pallas import tpu as pltpu
from jax.sharding import PartitionSpec as P

D = 960
HEADS = 15
KV_HEADS = 5
GROUP = 3
HEAD = 64
HALF = 32
FF = 2560
BLK = 64
L = 2048
CTX = 16
FS = 4
ROWS = 128
QKV = 1600
WIDE = 1664
SHARD = D // FS
FSL = FF // FS
TILE = 256
NT = L // TILE
EPS = 1e-05
THETA = 100000.0
SCALE = HEAD**-0.5
F32 = jnp.float32
BF16 = jnp.bfloat16
VMEM_BYTES = 56 * 1024 * 1024


def call(kernel, outs, args, smem=0, scratch=(), flops=0):
    specs = [pl.BlockSpec(memory_space=pltpu.SMEM)] * smem
    specs += [pl.BlockSpec(memory_space=pltpu.VMEM)] * (len(args) - smem)
    moved = sum(a.size * a.dtype.itemsize for a in list(args) + list(outs))
    return pl.pallas_call(
        kernel,
        out_shape=outs,
        in_specs=specs,
        out_specs=[pl.BlockSpec(memory_space=pltpu.VMEM)] * len(outs),
        scratch_shapes=list(scratch),
        cost_estimate=pl.CostEstimate(flops=flops, bytes_accessed=moved, transcendentals=0),
        compiler_params=pltpu.CompilerParams(vmem_limit_bytes=VMEM_BYTES),
    )(*args)


def shape(*dims, dtype=BF16):
    return jax.ShapeDtypeStruct(dims, dtype)


def dot(left, right, a=1, b=0):
    return lax.dot_general(left, right, (((a,), (b,)), ((), ())), preferred_element_type=F32)


def inv_norm(rows):
    return lax.rsqrt(jnp.mean(rows * rows, axis=-1, keepdims=True) + EPS)


def qkv_kernel(x_ref, w_ref, cos_ref, sin_ref, at_ref, out_ref, gains_ref):
    x = x_ref[...].astype(F32)
    gains = w_ref[:, WIDE - 128 : WIDE].astype(F32).T
    gains_ref[...] = gains[64:72, :]
    a = (x * inv_norm(x) * gains[64:65, :]).astype(BF16)
    at_ref[...] = a.astype(F32).T.astype(BF16)
    lin = dot(a, w_ref[...]).T
    cos = cos_ref[...]
    sin = sin_ref[...]

    def turned(base):
        first = lin[base : base + HALF]
        second = lin[base + HALF : base + HEAD]
        return jnp.concatenate(
            [first * cos - second * sin, second * cos + first * sin], axis=0
        ).astype(BF16)

    for j in range(KV_HEADS):
        key = turned(D + HEAD * j)
        value = lin[D + HEAD * (KV_HEADS + j) : D + HEAD * (KV_HEADS + j + 1)].astype(BF16)
        for g in range(GROUP):
            head = j * GROUP + g
            out_ref[head, 0:HEAD, :] = turned(HEAD * head)
            out_ref[head, HEAD : 2 * HEAD, :] = key
            out_ref[head, 2 * HEAD : 3 * HEAD, :] = value
    out_ref[HEADS, :, :] = jnp.zeros((3 * HEAD, ROWS), BF16)


def pick_pair(load, first, second):
    left = load(first // 2).astype(F32)
    right = load(second // 2).astype(F32)
    left = pltpu.roll(left, (first % 2) * BLK, 1)
    right = pltpu.roll(right, (1 - second % 2) * BLK, 1)
    lane = lax.broadcasted_iota(jnp.int32, left.shape, 1)
    return jnp.where(lane < BLK, left, right)


def causal(size):
    key = lax.broadcasted_iota(jnp.int32, (size, size), 0)
    query = lax.broadcasted_iota(jnp.int32, (size, size), 1)
    return key <= query


def attend_kernel(
    order_ref, inv_ref, recv_ref, out_ref, qt_ref, kt_ref, k_ref, vt_ref, of_ref, lse_ref, s_ref
):
    for m in range(CTX):
        got = pick_pair(lambda i: recv_ref[i], inv_ref[2 * m], inv_ref[2 * m + 1])
        at = slice(2 * BLK * m, 2 * BLK * (m + 1))
        qt_ref[:, at] = (got[0:HEAD] * SCALE).astype(BF16)
        key = got[HEAD : 2 * HEAD]
        kt_ref[:, at] = key.astype(BF16)
        k_ref[at, :] = key.T.astype(BF16)
        vt_ref[:, at] = got[2 * HEAD : 3 * HEAD].astype(BF16)
    allowed = causal(TILE)
    for n in range(NT):
        span = slice(TILE * n, TILE * (n + 1))
        query = qt_ref[:, span]
        top = None
        for c in range(n + 1):
            rows = slice(TILE * c, TILE * (c + 1))
            s = dot(k_ref[rows, :], query)
            if c == n:
                s = jnp.where(allowed, s, -1e30)
            s_ref[rows, :] = s
            part = jnp.max(s, axis=0, keepdims=True)
            top = part if top is None else jnp.maximum(top, part)
        total = None
        for c in range(n + 1):
            rows = slice(TILE * c, TILE * (c + 1))
            e = jnp.exp(s_ref[rows, :] - top)
            s_ref[rows, :] = e
            part = jnp.sum(e, axis=0, keepdims=True)
            total = part if total is None else total + part
        recip = 1.0 / total
        lse_ref[n] = jnp.broadcast_to(top + jnp.log(total), (8, TILE))
        prob = (s_ref[0 : TILE * (n + 1), :] * recip).astype(BF16)
        o = dot(vt_ref[:, 0 : TILE * (n + 1)], prob)
        of_ref[2 * n] = o[:, 0 : 2 * BLK]
        of_ref[2 * n + 1] = o[:, 2 * BLK :]
    for i in range(CTX):
        got = pick_pair(lambda g: of_ref[g], order_ref[2 * i], order_ref[2 * i + 1])
        out_ref[i] = got.astype(BF16)


def attend_back_kernel(
    order_ref,
    inv_ref,
    recv_ref,
    qt_ref,
    q_ref,
    kt_ref,
    k_ref,
    v_ref,
    of_ref,
    lse_ref,
    cos_ref,
    sin_ref,
    out_ref,
    dot_ref,
    do_ref,
    delta_ref,
    dk_ref,
    dv_ref,
    st_ref,
):
    for m in range(CTX):
        got = pick_pair(lambda i: recv_ref[i], inv_ref[2 * m], inv_ref[2 * m + 1])
        at = slice(2 * BLK * m, 2 * BLK * (m + 1))
        dot_ref[:, at] = got.astype(BF16)
        do_ref[at, :] = got.T.astype(BF16)
        delta_ref[:, at] = jnp.broadcast_to(
            jnp.sum(got * of_ref[m], axis=0, keepdims=True), (8, 2 * BLK)
        )
    allowed = causal(TILE)
    for n in range(NT):
        span = slice(TILE * n, TILE * (n + 1))
        query = qt_ref[:, span]
        out_grad = dot_ref[:, span]
        lse = lse_ref[n][0:1, :]
        delta = delta_ref[0:1, span]
        dq = None
        for c in range(n + 1):
            rows = slice(TILE * c, TILE * (c + 1))
            prob = jnp.exp(dot(k_ref[rows, :], query) - lse)
            if c == n:
                prob = jnp.where(allowed, prob, 0.0)
            ds = (prob * (dot(v_ref[rows, :], out_grad) - delta)).astype(BF16)
            part = dot(kt_ref[:, rows], ds)
            dq = part if dq is None else dq + part
            dk = dot(ds, q_ref[span, :])
            dv = dot(prob.astype(BF16), do_ref[span, :])
            if c == n:
                dk_ref[rows, :] = dk
                dv_ref[rows, :] = dv
            else:
                dk_ref[rows, :] += dk
                dv_ref[rows, :] += dv
        st_ref[2 * n, 0:HEAD, :] = dq[:, 0 : 2 * BLK] * SCALE
        st_ref[2 * n + 1, 0:HEAD, :] = dq[:, 2 * BLK :] * SCALE
    for m in range(CTX):
        at = slice(2 * BLK * m, 2 * BLK * (m + 1))
        cos = cos_ref[:, at]
        sin = sin_ref[:, at]

        def turned(value):
            first = value[0:HALF]
            second = value[HALF:HEAD]
            return jnp.concatenate(
                [first * cos + second * sin, second * cos - first * sin], axis=0
            )

        st_ref[m, 0:HEAD, :] = turned(st_ref[m, 0:HEAD, :])
        st_ref[m, HEAD : 2 * HEAD, :] = turned(dk_ref[at, :].T)
        st_ref[m, 2 * HEAD : 3 * HEAD, :] = dv_ref[at, :].T
    for i in range(CTX):
        got = pick_pair(lambda g: st_ref[g], order_ref[2 * i], order_ref[2 * i + 1])
        out_ref[i] = got.astype(BF16)


def resid_kernel(ot_ref, w_ref, x_ref, gains_ref, h_ref, b_ref, flat_ref):
    flat = jnp.concatenate([ot_ref[h] for h in range(HEADS)], axis=0)
    flat_ref[...] = flat
    mixed = flat.astype(F32).T.astype(BF16)
    h = x_ref[...].astype(F32) + dot(mixed, w_ref[...])
    h_ref[...] = h
    b_ref[...] = (h * inv_norm(h) * gains_ref[1:2, :]).astype(BF16)


def mlp_kernel(b_ref, g_ref, gu_ref, down_ref, y_ref, db_ref, mm_ref, dgu_ref):
    tokens = b_ref.shape[0] * ROWS
    for s in range(FS):
        b = b_ref[s]
        g = g_ref[s]
        gu = dot(b, gu_ref[...])
        gate = gu[:, :FSL]
        up = gu[:, FSL:]
        sig = 1.0 / (1.0 + jnp.exp(-gate))
        act = gate * sig
        mm = (act * up).astype(BF16)
        dm = dot(g, down_ref[...], 1, 1)
        dgate = dm * up * sig * (1.0 + gate * (1.0 - sig))
        dgu = jnp.concatenate([dgate, dm * act], axis=1).astype(BF16)
        rows = slice(ROWS * s, ROWS * (s + 1))
        mm_ref[rows, :] = mm
        dgu_ref[rows, :] = dgu
        db_ref[s] = dot(dgu, gu_ref[...], 1, 1).astype(BF16)
        y_ref[s] = dot(mm, down_ref[...]).astype(BF16)


def mlp_grad_kernel(b_ref, g_ref, mm_ref, dgu_ref, dgu_w_ref, dd_w_ref):
    b = b_ref[...].reshape(FS * ROWS, D)
    dgu_w_ref[...] = dot(b, dgu_ref[...], 0, 0).astype(BF16)
    dd_w_ref[...] = dot(mm_ref[...], g_ref[...].reshape(FS * ROWS, D), 0, 0).astype(BF16)


def mid_kernel(db0, db1, db2, db3, h_ref, g_ref, gains_ref, w_ref, dh_ref, e_ref, do_ref, dg_ref):
    db = db0[...].astype(F32) + db1[...].astype(F32) + db2[...].astype(F32) + db3[...].astype(F32)
    h = h_ref[...]
    r2 = inv_norm(h)
    dg_ref[...] = jnp.broadcast_to(jnp.sum(db * h * r2, axis=0, keepdims=True), (8, D))
    scaled = gains_ref[1:2, :] * db
    dh = (
        g_ref[...].astype(F32)
        + r2 * scaled
        - h * (r2 * r2 * r2) * jnp.mean(scaled * h, axis=-1, keepdims=True)
    )
    dh_ref[...] = dh
    e = dh.astype(BF16)
    e_ref[...] = e
    back = dot(w_ref[...], e, 1, 1).astype(BF16)
    for head in range(HEADS):
        do_ref[head] = back[HEAD * head : HEAD * (head + 1)]
    do_ref[HEADS] = jnp.zeros((HEAD, ROWS), BF16)


def out_grad_kernel(ot_ref, e_ref, out_ref):
    total = dot(ot_ref[0], e_ref[0])
    for f in range(1, FS):
        total += dot(ot_ref[f], e_ref[f])
    out_ref[...] = total.astype(BF16)


def last_kernel(recv_ref, w_ref, x_ref, dh_ref, gains_ref, dg2_ref, ig_ref, msg_ref):
    for head in range(HEADS):
        msg_ref[HEAD * head : HEAD * (head + 1), :] = recv_ref[head, 0:HEAD, :]
    for part in range(2):
        for j in range(KV_HEADS):
            total = None
            for g in range(GROUP):
                piece = recv_ref[j * GROUP + g, HEAD * (part + 1) : HEAD * (part + 2), :]
                piece = piece.astype(F32)
                total = piece if total is None else total + piece
            base = D + HEAD * (KV_HEADS * part + j)
            msg_ref[base : base + HEAD, :] = total.astype(BF16)
    da = dot(w_ref[:, 0:QKV], msg_ref[0:QKV, :]).T
    x = x_ref[...].astype(F32)
    r1 = inv_norm(x)
    dg1 = jnp.sum(da * x * r1, axis=0, keepdims=True)
    scaled = gains_ref[0:1, :] * da
    ig_ref[...] = (
        dh_ref[...]
        + r1 * scaled
        - x * (r1 * r1 * r1) * jnp.mean(scaled * x, axis=-1, keepdims=True)
    )
    pad = jnp.zeros((1, 1024 - D), F32)
    rows = []
    for row in (dg1, dg2_ref[0:1, :]):
        full = jnp.concatenate([row, pad], axis=1)
        rows += [full[:, 128 * i : 128 * (i + 1)] for i in range(8)]
    msg_ref[QKV : QKV + 16, :] = jnp.concatenate(rows, axis=0).astype(BF16)


def qkv_grad_kernel(at_ref, d_ref, out_ref):
    total = dot(at_ref[0], d_ref[0, 0:QKV, :], 1, 1)
    gains = d_ref[0, QKV : QKV + 16, :].astype(F32)
    for f in range(1, FS):
        total += dot(at_ref[f], d_ref[f, 0:QKV, :], 1, 1)
        gains += d_ref[f, QKV : QKV + 16, :].astype(F32)
    out_ref[0:SHARD, 0:QKV] = total.astype(BF16)
    out_ref[0:SHARD, QKV:WIDE] = jnp.zeros((SHARD, WIDE - QKV), BF16)
    rows = []
    for part in range(2):
        row = [gains[8 * part + i : 8 * part + i + 1, :] for i in range(8)]
        rows.append(jnp.concatenate(row + [jnp.zeros((1, WIDE - 1024), F32)], axis=1))
    rows.append(jnp.zeros((14, WIDE), F32))
    out_ref[SHARD : SHARD + 16, :] = jnp.concatenate(rows, axis=0).astype(BF16)


def swap_core(value):
    return lax.ppermute(value, "ctx", [(i, i ^ 1) for i in range(CTX)])


def shift(value, step):
    return lax.ppermute(value, "fsdp", [((i + step) % FS, i) for i in range(FS)])


def to_all(value, axis, count):
    return lax.all_to_all(jnp.broadcast_to(value[None], (count,) + value.shape), axis, 0, 0)


def gather_weights(shard):
    core = lax.axis_index("ctx") % 2
    half = shard.shape[0] // 2
    mine = to_all(lax.dynamic_slice_in_dim(shard, core * half, half, 0), "fsdp", FS)
    other = swap_core(mine)
    low = jnp.where(core == 0, mine, other)
    high = jnp.where(core == 0, other, mine)
    return jnp.concatenate([low, high], axis=1).reshape((2 * FS * half,) + shard.shape[1:])


def gather_rolled(value):
    return jnp.stack([value] + [shift(value, s) for s in range(1, FS)])


def scatter_rolled(pieces):
    return [pieces[0]] + [shift(pieces[s], -s) for s in range(1, FS)]


def shards(tokens, gain_attn, w_q, w_kv, w_o, gain_mlp, w_gate_up, w_down, block_order, cotangent):
    x = tokens[0]
    g_own = cotangent[0]
    order = block_order[0]
    place = lax.axis_index("ctx")
    fs = lax.axis_index("fsdp")

    slots = jnp.arange(2 * CTX, dtype=jnp.int32)
    inverse = jnp.sum(jnp.where(order[None, :] == slots[:, None], slots[None, :], 0), axis=1)
    mine = lax.dynamic_slice_in_dim(order, place * 2, 2)
    places = (mine[:, None] * BLK + jnp.arange(BLK, dtype=jnp.int32)[None, :]).reshape(ROWS)
    freq = THETA ** (-(jnp.arange(HALF, dtype=F32) * 2.0 / HEAD))
    angle = freq[:, None] * places.astype(F32)[None, :]
    angle_all = freq[:, None] * jnp.arange(L, dtype=F32)[None, :]

    message = jnp.concatenate(
        [w_q, w_kv, gain_attn[:, None], gain_mlp[:, None], jnp.zeros((SHARD, 62), BF16)], axis=1
    )
    w_qkv = gather_weights(message)
    w_out = lax.all_gather(w_o, "fsdp", axis=0, tiled=True)
    chunks = w_gate_up.reshape(SHARD, 2, FS, FSL).transpose(2, 0, 1, 3).reshape(FS, SHARD, 2 * FSL)
    chunks = jnp.roll(chunks, -fs, axis=0)
    pieces = scatter_rolled([chunks[s] for s in range(FS)])
    w_gu = jnp.roll(
        jnp.stack([pieces[0], pieces[3], pieces[2], pieces[1]]), fs, axis=0
    ).reshape(D, 2 * FSL)
    g_all = gather_rolled(g_own)

    a_t, packed, gains = call(
        qkv_kernel,
        [shape(D, ROWS), shape(CTX, 3 * HEAD, ROWS), shape(8, D, dtype=F32)],
        [x, w_qkv, jnp.cos(angle), jnp.sin(angle)],
        flops=2 * ROWS * D * QKV,
    )
    received = lax.all_to_all(packed, "ctx", 0, 0)
    o_part, q_t, k_t, k_n, v_t, o_f, lse = call(
        attend_kernel,
        [
            shape(CTX, HEAD, ROWS),
            shape(HEAD, L),
            shape(HEAD, L),
            shape(L, HEAD),
            shape(HEAD, L),
            shape(CTX, HEAD, ROWS, dtype=F32),
            shape(NT, 8, TILE, dtype=F32),
        ],
        [order, inverse, received],
        smem=2,
        scratch=[pltpu.VMEM((L, TILE), F32)],
        flops=2 * L * L * HEAD,
    )
    o_all = lax.all_to_all(o_part, "ctx", 0, 0)
    h, b, o_flat = call(
        resid_kernel,
        [shape(ROWS, D, dtype=F32), shape(ROWS, D), shape(D, ROWS)],
        [o_all, w_out, x, gains],
        flops=2 * ROWS * D * D,
    )
    a_all = lax.all_gather(a_t, "fsdp", axis=0)
    o_flat_all = lax.all_gather(o_flat, "fsdp", axis=0)
    b_all = gather_rolled(b)
    y_part, db_part, mm, dgu = call(
        mlp_kernel,
        [shape(FS, ROWS, D), shape(FS, ROWS, D), shape(FS * ROWS, FSL), shape(FS * ROWS, 2 * FSL)],
        [b_all, g_all, w_gu, w_down],
        flops=12 * FS * ROWS * D * FSL,
    )
    db = scatter_rolled([db_part[s] for s in range(FS)])
    y = scatter_rolled([y_part[s] for s in range(FS)])
    gu_grad, down_grad = call(
        mlp_grad_kernel,
        [shape(D, 2 * FSL), shape(FSL, D)],
        [b_all, g_all, mm, dgu],
        flops=6 * FS * ROWS * D * FSL,
    )
    dh, e, do_part, dgain_two = call(
        mid_kernel,
        [
            shape(ROWS, D, dtype=F32),
            shape(ROWS, D),
            shape(CTX, HEAD, ROWS),
            shape(8, D, dtype=F32),
        ],
        [db[0], db[1], db[2], db[3], h, g_own, gains, w_out],
        flops=2 * ROWS * D * D,
    )
    do_all = lax.all_to_all(do_part, "ctx", 0, 0)
    e_all = lax.all_gather(e, "fsdp", axis=0)
    result = h
    for piece in y:
        result = result + piece.astype(F32)
    (dqkv_part,) = call(
        attend_back_kernel,
        [shape(CTX, 3 * HEAD, ROWS)],
        [
            order,
            inverse,
            do_all,
            q_t,
            q_t.T,
            k_t,
            k_n,
            v_t.T,
            o_f,
            lse,
            jnp.cos(angle_all),
            jnp.sin(angle_all),
        ],
        smem=2,
        scratch=[
            pltpu.VMEM((HEAD, L), BF16),
            pltpu.VMEM((L, HEAD), BF16),
            pltpu.VMEM((8, L), F32),
            pltpu.VMEM((L, HEAD), F32),
            pltpu.VMEM((L, HEAD), F32),
            pltpu.VMEM((CTX, 3 * HEAD, ROWS), F32),
        ],
        flops=5 * L * L * HEAD,
    )
    gu_grad = lax.all_to_all(gu_grad.reshape(FS, SHARD, 2 * FSL), "fsdp", 0, 0)
    (o_grad,) = call(
        out_grad_kernel,
        [shape(SHARD, D)],
        [lax.dynamic_slice_in_dim(o_flat_all, fs * SHARD, SHARD, 1), e_all],
        flops=2 * FS * ROWS * SHARD * D,
    )
    gu_sum, down_sum, o_sum = (
        lax.psum(part, ("seq", "ctx")) for part in (gu_grad, down_grad, o_grad)
    )

    dqkv = lax.all_to_all(dqkv_part, "ctx", 0, 0)
    input_grad, low = call(
        last_kernel,
        [shape(ROWS, D, dtype=F32), shape(QKV + 16, ROWS)],
        [dqkv, w_qkv, x, dh, gains, dgain_two],
        flops=2 * ROWS * D * QKV,
    )
    low_all = to_all(low, "fsdp", FS)
    (grads,) = call(
        qkv_grad_kernel,
        [shape(SHARD + 16, WIDE)],
        [lax.dynamic_slice_in_dim(a_all, fs * SHARD, SHARD, 1), low_all],
        flops=2 * FS * ROWS * SHARD * QKV,
    )
    parts = lax.all_to_all(grads.reshape(32, 8, WIDE), ("seq", "ctx"), 0, 0)
    summed = jnp.sum(parts.astype(F32), axis=0).astype(BF16)
    grads = to_all(summed, ("seq", "ctx"), 32).reshape(SHARD + 16, WIDE).astype(F32)
    own_gains = lax.dynamic_slice(grads, (SHARD, fs * SHARD), (2, SHARD))
    gu_out = gu_sum.reshape(FS, SHARD, 2, FSL).transpose(1, 2, 0, 3).reshape(SHARD, 2 * FF)
    return (
        result.astype(BF16)[None],
        input_grad[None],
        own_gains[0],
        grads[:SHARD, :D],
        grads[:SHARD, D:QKV],
        o_sum.astype(F32),
        own_gains[1],
        gu_out.astype(F32),
        down_sum.astype(F32),
    )


def solution(mesh):
    tokens = P(("seq", "fsdp"), "ctx", None)
    return jax.shard_map(
        shards,
        mesh=mesh,
        in_specs=(
            tokens,
            P("fsdp"),
            P("fsdp", None),
            P("fsdp", None),
            P("fsdp", None),
            P("fsdp"),
            P("fsdp", None),
            P("fsdp", None),
            P(("seq", "fsdp"), None),
            tokens,
        ),
        out_specs=(
            tokens,
            tokens,
            P("fsdp"),
            P("fsdp", None),
            P("fsdp", None),
            P("fsdp", None),
            P("fsdp"),
            P("fsdp", None),
            P("fsdp", None),
        ),
        check_vma=False,
    )
```

time: 928 us -> 465 us (0.50)
  waiting for transfers between devices: 560 us -> 141 us
  matrix products: 123 us -> 0 us
  Pallas kernels: 0 us -> 59.7 us
  starting transfers between devices: 0.82 us -> 59.6 us
  local copies, waits for them, and re-layouts: 97.4 us -> 46.4 us
  blocking collectives: 81.1 us -> 108 us
    all_gather x7 -> x1, waiting for transfers between devices: 235 us -> 0.01 us  [shards(): w_out = lax.all_gather(w_o, 'fsdp', axis=0, tiled=True)]
    reduce_scatter x4 -> x0, waiting for transfers between devices: 181 us -> none  [the longest x1 95.8 us: shards(): lax.psum_scatter(grad_gu.astype(jnp.bfloat16), 'fsdp', scatter_dimension=...]
    dot_general x78 -> x0, matrix products: 123 us -> none  [the longest x9 19.6 us: weigh(): jnp.einsum('jgtk,kje->tjge', probs, value_block, preferred_element_type=F...]
    unnamed x16 -> x2, waiting for transfers between devices: 108 us -> 0.03 us
    psum x1 -> x0, blocking collectives: 65 us -> none  [shards(): lax.psum(shard_grads[0].astype(jnp.bfloat16), ('seq', 'ctx'))]
    pallas_call x0 -> x10, Pallas kernels: none -> 59.7 us  [call(): pl.pallas_call(kernel, out_shape=outs, in_specs=specs, out_specs=[pl.Bloc...]
    all_to_all x0 -> x2, blocking collectives: none -> 56.5 us  [the longest x1 31.4 us: shards(): parts = lax.all_to_all(grads.reshape(32, 8, WIDE), ('seq', 'ctx'), 0, 0)]
    all_gather x0 -> x3, blocking collectives: none -> 51.6 us  [the longest x1 27.7 us: shards(): o_flat_all = lax.all_gather(o_flat, 'fsdp', axis=0)]
  transfers between devices with their start and end apart: 14 -> 25, of which waited for: 13 -> 13; matrix products, arithmetic and copies ran while one was open for 14% -> 12% of each run, Pallas kernels for 0% -> 7%
where the time goes in v1:
time: 465 us; the launch traced here: 456 us
  waiting for transfers between devices  141 us (30%)
  blocking collectives  108 us (23%)
  Pallas kernels  59.7 us (13%)
  starting transfers between devices  59.6 us (13%)
  local copies, waits for them, and re-layouts  46.4 us (10%)
  other arithmetic  26.9 us (6%)
  between operations  14.8 us (3%)
    pallas_call x10, Pallas kernels, call(): pl.pallas_call(kernel, out_shape=outs, in_specs=specs, out_specs=[pl.Bloc...  59.7 us
    psum x1, waiting for transfers between devices, shards(): lax.psum(part, ('seq', 'ctx'))  54.7 us
    ppermute x15, waiting for transfers between devices, shift(): lax.ppermute(value, 'fsdp', [((i + step) % FS, i) for i in range(FS)])  43.4 us
    all_to_all x1, blocking collectives, shards(): parts = lax.all_to_all(grads.reshape(32, 8, WIDE), ('seq', 'ctx'), 0, 0)  31.4 us
    all_gather x1, blocking collectives, shards(): o_flat_all = lax.all_gather(o_flat, 'fsdp', axis=0)  27.7 us
    all_to_all x1, blocking collectives, to_all(): lax.all_to_all(jnp.broadcast_to(value[None], (count,) + value.shape), axi...  25.1 us
    all_to_all x1, waiting for transfers between devices, shards(): gu_grad = lax.all_to_all(gu_grad.reshape(FS, SHARD, 2 * FSL), 'fsdp', 0, 0)  24.9 us
    ppermute x15, starting transfers between devices, shift(): lax.ppermute(value, 'fsdp', [((i + step) % FS, i) for i in range(FS)])  20.2 us
  transfers between devices with their start and end apart: 25, of which 13 were waited for; matrix products, arithmetic and copies ran while one was open for 12% of the time, Pallas kernels for 7%

profile of v1, /device:TPU:1, one launch (start us, length us, event | category | flops | bytes accessed | tf_op | source)
XLA Modules:
  0.0 456.5 jit_solution(6728336313148246027)
XLA Ops:
  10.5 25.1 %all_to_all.45 = bf16[4,120,1664]{2,1,0:T(8,128)(2,1)} all-to-all(bf16[4,120,1664]{2,1,0:T(8,128)(2,1)S(1)} %broadcast_in_dim.58), channel_id=1, replica_groups=mesh['seq'=2,'ctx'=16,'fsdp'=4] {'fsdp'}, dimensions={0} | all-to-all | bytes 3194880 | tf_op jit(solution)/shard_map/all_to_all | solution.py:341
  39.3 3.0 reshape.83
  42.3 3.6 copy.48
  45.9 2.8 reshape.84
  49.5 2.6 fusion.7
  56.2 3.6 shard_map.169
  59.8 8.1 %all-to-all-start.1 = ((bf16[16,192,128]{2,1,0:T(8,128)(2,1)}), bf16[16,192,128]{2,1,0:T(8,128)(2,1)}, u32[]{:S(2)}, u32[]{:S(2)}) async-start(bf16[16,192,128]{2,1,0:T(8,128)(2,1)} %get-tuple-element.35), calls=%async_computation.1 | async-start | bytes 1572864 | tf_op jit(solution)/shard_map/all_to_all | solution.py:396
  69.2 2.4 collective-permute-start.7
  72.2 2.4 collective-permute-start.5
  74.6 2.5 collective-permute-start.4
  77.7 4.7 %all-to-all-done.1.recv_ref = bf16[16,192,128]{2,1,0:T(8,128)(2,1)} async-done(((bf16[16,192,128]{2,1,0:T(8,128)(2,1)}), bf16[16,192,128]{2,1,0:T(8,128)(2,1)}, u32[]{:S(2)}, u32[]{:S(2)}) %all-to-all-start.1) | async-done | bytes 786464 | tf_op jit(solution)/shard_map/all_to_all | solution.py:396
  82.5 7.9 %shard_map.170 = (bf16[16,64,128]{2,1,0:T(8,128)(2,1)}, bf16[64,2048]{1,0:T(8,128)(2,1)}, bf16[64,2048]{1,0:T(8,128)(2,1)}, bf16[2048,64]{1,0:T(8,128)(2,1)}, bf...) custom-call(s32[32]{0:T(128)} %bitcast.87, s32[32]{0:T(128)} %select_reduce_fusion.inv_ref, ...), custom_call_target="tpu_custom_call" | custom-call | flops 536870912 | bytes 2687232 | tf_op jit(solution)/shard_map/pallas_call | solution.py:40
  90.3 4.2 all-to-all-start.2
  96.5 10.6 %collective-permute-done.5 = bf16[128,960]{1,0:T(8,128)(2,1)S(1)} collective-permute-done((bf16[128,960]{1,0:T(8,128)(2,1)S(1)}, bf16[128,960]{1,0:T(8,128)(2,1)S(1)}, u32[]{:S(2)}, u32[]{:S(2)}) %collective-permute-start.5) | collective-permute-done | bytes 245792 | tf_op jit(solution)/shard_map/ppermute | solution.py:337
  112.2 3.1 shard_map.171
  115.3 4.6 %collective-permute-start.2 = (bf16[128,960]{1,0:T(8,128)(2,1)}, bf16[128,960]{1,0:T(8,128)(2,1)S(1)}, u32[]{:S(2)}, u32[]{:S(2)}) collective-permute-start(bf16[128,960]{1,0:T(8,128)(2,1)} %get-tuple-element.39), channel_id=1, source_target_pairs={{2,0},{3,1},{0,2},{1,3},{6,4},{7,5},{4,6},{5,7},{10,8},{11,9},{8,1... | collective-permute-start | bytes 737288 | tf_op jit(solution)/shard_map/ppermute | solution.py:337
  120.2 5.3 %fusion.3 = bf16[4,240,1280]{2,1,0:T(8,128)(2,1)} fusion(s32[]{:T(128)S(6)} %select_n.59, bf16[1,240,1280]{2,1,0:T(8,128)(2,1)S(1)} %get-tuple-element.95, bf16[1,240,1280]{2,1,0:T(8,128)(2,1)S(1)} %bitcast.76, bf16[1,240,1280]{2,1,0:T(8,128)(2,1)} %bitcast.16, bf16[1,240,1280]{2,1,0:T(8,128)(2,1)} %bitcast.18), kind=kLoop, calls=%fused_computation.14 | loop fusion | flops 8601600 | bytes 4915204 | tf_op jit(solution)/shard_map/jit(_roll_dynamic)/concatenate | solution.py:385
  125.5 5.7 %collective-permute-done.2 = bf16[128,960]{1,0:T(8,128)(2,1)S(1)} collective-permute-done((bf16[128,960]{1,0:T(8,128)(2,1)}, bf16[128,960]{1,0:T(8,128)(2,1)S(1)}, u32[]{:S(2)}, u32[]{:S(2)}) %collective-permute-start.2) | collective-permute-done | bytes 245792 | tf_op jit(solution)/shard_map/ppermute | solution.py:337
  132.4 10.9 %shard_map.172 = (bf16[4,128,960]{2,1,0:T(8,128)(2,1)}, bf16[4,128,960]{2,1,0:T(8,128)(2,1)}, bf16[512,640]{1,0:T(8,128)(2,1)}, bf16[512,1280]{1,0:T(8,128)(2,1)}) custom-call(bf16[4,128,960]{2,1,0:T(8,128)(2,1)} %pad_maximum_fusion.1.b_ref, bf16[4,128,960]{2,1,0:T(8,128)(2,1)} %pad_maximum_fusion.2.g_ref, bf16[960,1280]{1,0:T(8,128)(2,1)} %bitcast.68, ...), custom_call_target="tpu_custom_call" | custom-call | flops 3774873600 | bytes 9584640 | tf_op jit(solution)/shard_map/pallas_call | solution.py:40
  146.9 2.7 collective-permute-start.14
  149.6 3.8 collective-permute-done.13.db1
  153.4 7.7 %collective-permute-done.14.db2 = bf16[128,960]{1,0:T(8,128)(2,1)S(1)} collective-permute-done((bf16[128,960]{1,0:T(8,128)(2,1)S(1)}, bf16[128,960]{1,0:T(8,128)(2,1)S(1)}, u32[]{:S(2)}, u32[]{:S(2)}) %collective-permute-start.14) | collective-permute-done | bytes 245792 | tf_op jit(solution)/shard_map/ppermute | solution.py:337
  162.0 3.9 shard_map.173
  165.9 8.3 %all-to-all-start.3 = ((bf16[16,64,128]{2,1,0:T(8,128)(2,1)}), bf16[16,64,128]{2,1,0:T(8,128)(2,1)S(1)}, u32[]{:S(2)}, u32[]{:S(2)}) async-start(bf16[16,64,128]{2,1,0:T(8,128)(2,1)} %get-tuple-element.42), calls=%async_computation.3 | async-start | bytes 524288 | tf_op jit(solution)/shard_map/all_to_all | solution.py:448
  178.0 4.7 %all-to-all-done.3.recv_ref = bf16[16,64,128]{2,1,0:T(8,128)(2,1)S(1)} async-done(((bf16[16,64,128]{2,1,0:T(8,128)(2,1)}), bf16[16,64,128]{2,1,0:T(8,128)(2,1)S(1)}, u32[]{:S(2)}, u32[]{:S(2)}) %all-to-all-start.3) | async-done | bytes 262176 | tf_op jit(solution)/shard_map/all_to_all | solution.py:448
  183.4 13.6 %shard_map.174 = bf16[16,192,128]{2,1,0:T(8,128)(2,1)} custom-call(s32[32]{0:T(128)} %bitcast.88, s32[32]{0:T(128)} %select_reduce_fusion.inv_ref, bf16[16,64,128]{2,1,0:T(8,128)(2,1)} %copy-done.13, bf16[64,2048]{1,0:T(8,128)(2,1)} %get-tuple-element.43.qt_ref, bf16[2048,64]{1,0:T(8,128)(2,1)} %bitcast.77, bf16[64,2048]{1,0:T(8,128)(2,1)} %get-tuple-element.44.kt_ref, ...), custom_call_target="tpu_custom_call" | custom-call | flops 1342177280 | bytes 3473664 | tf_op jit(solution)/shard_map/pallas_call | solution.py:40
  197.0 4.7 %all-to-all-start.4 = ((bf16[16,192,128]{2,1,0:T(8,128)(2,1)}), bf16[16,192,128]{2,1,0:T(8,128)(2,1)S(1)}, u32[]{:S(2)}, u32[]{:S(2)}) async-start(bf16[16,192,128]{2,1,0:T(8,128)(2,1)} %shard_map.174), calls=%async_computation.4 | async-start | bytes 1572864 | tf_op jit(solution)/shard_map/all_to_all | solution.py:492
  201.7 5.9 %shard_map.178 = (bf16[960,1280]{1,0:T(8,128)(2,1)}, bf16[640,960]{1,0:T(8,128)(2,1)}) custom-call(bf16[4,128,960]{2,1,0:T(8,128)(2,1)} %pad_maximum_fusion.1.b_ref, bf16[4,128,960]{2,1,0:T(8,128)(2,1)} %pad_maximum_fusion.2.g_ref, bf16[512,640]{1,0:T(8,128)(2,1)} %get-tuple-element.56.mm_ref, bf16[512,1280]{1,0:T(8,128)(2,1)} %get-tuple-element.57.dgu_ref), custom_call_target="tpu_custom_call" | custom-call | flops 1887436800 | bytes 7618560 | tf_op jit(solution)/shard_map/pallas_call | solution.py:40
  207.6 8.5 %all-to-all-done.4.recv_ref = bf16[16,192,128]{2,1,0:T(8,128)(2,1)S(1)} async-done(((bf16[16,192,128]{2,1,0:T(8,128)(2,1)}), bf16[16,192,128]{2,1,0:T(8,128)(2,1)S(1)}, u32[]{:S(2)}, u32[]{:S(2)}) %all-to-all-start.4) | async-done | bytes 786464 | tf_op jit(solution)/shard_map/all_to_all | solution.py:492
  217.0 3.6 all-to-all-start.8
  220.6 4.4 shard_map.175
  225.0 24.9 %all-to-all-done.8 = bf16[4,240,1280]{2,1,0:T(8,128)(2,1)S(1)} async-done(((bf16[4,240,1280]{2,1,0:T(8,128)(2,1)}), bf16[4,240,1280]{2,1,0:T(8,128)(2,1)S(1)}, u32[]{:S(2)}, u32[]{:S(2)}) %all-to-all-start.8) | async-done | bytes 2457632 | tf_op jit(solution)/shard_map/all_to_all | solution.py:481
  250.0 2.4 broadcast_in_dim.61
  252.4 4.5 all-to-all-start.5
  257.0 27.7 %all-gather.1 = bf16[3840,128]{1,0:T(8,128)(2,1)S(1)} all-gather(bf16[960,128]{1,0:T(8,128)(2,1)S(1)} %copy-done.19), channel_id=3, replica_groups=mesh['seq'=2,'ctx'=16,'fsdp'=4] {'fsdp'}, dimensions={0}, use_global_device_ids=true | all-gather | bytes 1228800 | tf_op jit(solution)/shard_map/all_gather | solution.py:421
  285.4 13.1 %all-gather.2 = bf16[512,960]{1,0:T(8,128)(2,1)} all-gather(bf16[128,960]{1,0:T(8,128)(2,1)S(1)} %copy-done.11), channel_id=4, replica_groups=mesh['seq'=2,'ctx'=16,'fsdp'=4] {'fsdp'}, dimensions={0}, use_global_device_ids=true | all-gather | bytes 1228800 | tf_op jit(solution)/shard_map/all_gather | solution.py:449
  298.5 2.8 shard_map.177
  303.4 3.6 copy.57
  307.0 3.0 convert_element_type.67
  311.0 10.8 %all-gather = bf16[3840,128]{1,0:T(8,128)(2,1)S(1)} all-gather(bf16[960,128]{1,0:T(8,128)(2,1)S(1)} %copy-done.18), channel_id=2, replica_groups=mesh['seq'=2,'ctx'=16,'fsdp'=4] {'fsdp'}, dimensions={0}, use_global_device_ids=true | all-gather | bytes 1228800 | tf_op jit(solution)/shard_map/all_gather | solution.py:420
  322.5 3.6 shard_map.176
  326.1 31.4 %all_to_all.46 = bf16[32,8,1664]{2,1,0:T(8,128)(2,1)S(1)} all-to-all(bf16[32,8,1664]{2,1,0:T(8,128)(2,1)} %bitcast.67), channel_id=1, replica_groups=mesh['seq'=2,'ctx'=16,'fsdp'=4] {'seq','ctx'}, dimensions={0} | all-to-all | bytes 1703936 | tf_op jit(solution)/shard_map/all_to_all | solution.py:506
  358.6 3.8 all-to-all-start.7
  366.1 5.1 %collective-permute-done.12 = bf16[128,960]{1,0:T(8,128)(2,1)S(1)} collective-permute-done((bf16[128,960]{1,0:T(8,128)(2,1)}, bf16[128,960]{1,0:T(8,128)(2,1)S(1)}, u32[]{:S(2)}, u32[]{:S(2)}) %collective-permute-start.12) | collective-permute-done | bytes 245792 | tf_op jit(solution)/shard_map/ppermute | solution.py:337
  371.2 2.3 collective-permute-done.11
  374.2 5.8 %collective-permute-done.10 = bf16[128,960]{1,0:T(8,128)(2,1)} collective-permute-done((bf16[128,960]{1,0:T(8,128)(2,1)}, bf16[128,960]{1,0:T(8,128)(2,1)}, u32[]{:S(2)}, u32[]{:S(2)}) %collective-permute-start.10) | collective-permute-done | bytes 245792 | tf_op jit(solution)/shard_map/ppermute | solution.py:337
  383.1 54.7 %all-reduce.3.cloned.1.call-done = (bf16[640,960]{1,0:T(8,128)(2,1)}, bf16[240,960]{1,0:T(8,128)(2,1)}, bf16[240,5120]{1,0:T(8,128)(2,1)}) async-done(((bf16[640,960]{1,0:T(8,128)(2,1)}, bf16[240,960]{1,0:T(8,128)(2,1)}, bf16[240,5120]{1,0:T(8,128)(2,1)}), (bf16[640,960]{1,0:T(8,128)(2,1)}, bf16[240,960]{1,0:T(8,128)(2,1)}, bf16[240,5120]{1,0:T(8,128)(2,1)})) %all-reduce.3.cloned.1.call-update) | async-done | bytes 4147216 | tf_op jit(solution)/shard_map/psum | solution.py:489
  439.9 4.6 %convert_element_type.68 = f32[240,5120]{1,0:T(8,128)} convert(bf16[240,5120]{1,0:T(8,128)(2,1)} %get-tuple-element.89) | non-fusion elementwise | flops 1228800 | bytes 7372800 | tf_op jit(solution)/shard_map/convert_element_type | solution.py:519
  (113 shorter events, 52.2 us)
Async XLA Ops:
  7.2 104.3 %all-gather.5.cloned.1.call-start = ((), (), s32[]{:S(2)}) async-start(), calls=%async_computation.9 | async-start | bytes 2457600 | tf_op jit(solution)/shard_map/all_gather | solution.py:381
  10.3 27.3 %copy-start.20 = (bf16[1,128,960]{1,2,0:T(8,128)(2,1)S(1)}, bf16[1,128,960]{1,2,0:T(8,128)(2,1)}, u32[]{:S(2)}) copy-start(bf16[1,128,960]{1,2,0:T(8,128)(2,1)} %param.21) | copy-start | bytes 737284
  10.5 27.7 %copy-start.21 = (bf16[1,128,960]{1,2,0:T(8,128)(2,1)S(1)}, bf16[1,128,960]{1,2,0:T(8,128)(2,1)}, u32[]{:S(2)}) copy-start(bf16[1,128,960]{1,2,0:T(8,128)(2,1)} %param.12) | copy-start | bytes 737284
  10.5 28.5 %copy-start.22 = (s32[1,32]{1,0:T(1,128)S(1)}, s32[1,32]{1,0:T(1,128)}, u32[]{:S(2)}) copy-start(s32[1,32]{1,0:T(1,128)} %param.20) | copy-start | bytes 388
  10.5 28.8 %copy-start.1 = (bf16[240,5120]{1,0:T(8,128)(2,1)S(1)}, bf16[240,5120]{1,0:T(8,128)(2,1)}, u32[]{:S(2)}) copy-start(bf16[240,5120]{1,0:T(8,128)(2,1)} %param.18) | copy-start | bytes 7372804
  35.6 16.4 %collective-permute-start = (bf16[4,120,1664]{2,1,0:T(8,128)(2,1)}, bf16[4,120,1664]{2,1,0:T(8,128)(2,1)}, u32[]{:S(2)}, u32[]{:S(2)}) collective-permute-start(bf16[4,120,1664]{2,1,0:T(8,128)(2,1)} %all_to_all.45), channel_id=1, source_target_pairs={{0,4},{4,0},{8,12},{12,8},{16,20},{20,16},{24,28},{28,24},{32,36},... | collective-permute-start | bytes 4792328 | tf_op jit(solution)/shard_map/ppermute | solution.py:333
  37.8 71.5 %copy-start.2 = (bf16[1,128,960]{2,1,0:T(8,128)(2,1)}, bf16[1,128,960]{2,1,0:T(8,128)(2,1)S(1)}, u32[]{:S(2)}) copy-start(bf16[1,128,960]{2,1,0:T(8,128)(2,1)S(1)} %copy.47) | copy-start | bytes 737284
  37.8 36.8 %collective-permute-start.6 = (bf16[128,960]{1,0:T(8,128)(2,1)S(1)}, bf16[128,960]{1,0:T(8,128)(2,1)}, u32[]{:S(2)}, u32[]{:S(2)}) collective-permute-start(bf16[128,960]{1,0:T(8,128)(2,1)S(1)} %bitcast.70), channel_id=1, source_target_pairs={{3,0},{0,1},{1,2},{2,3},{7,4},{4,5},{5,6},{6,7},{11,8},{8,9},{9,10... | collective-permute-start | bytes 737288 | tf_op jit(solution)/shard_map/ppermute | solution.py:337
  59.8 22.6 %all-to-all-start.1 = ((bf16[16,192,128]{2,1,0:T(8,128)(2,1)}), bf16[16,192,128]{2,1,0:T(8,128)(2,1)}, u32[]{:S(2)}, u32[]{:S(2)}) async-start(bf16[16,192,128]{2,1,0:T(8,128)(2,1)} %get-tuple-element.35), calls=%async_computation.1 | async-start | bytes 1572864 | tf_op jit(solution)/shard_map/all_to_all | solution.py:396
  69.2 25.3 %copy-start.5 = (bf16[640,960]{0,1:T(8,128)(2,1)S(1)}, bf16[640,960]{0,1:T(8,128)(2,1)}, u32[]{:S(2)}) copy-start(bf16[640,960]{0,1:T(8,128)(2,1)} %param.19) | copy-start | bytes 3686404
  69.2 50.8 %collective-permute-start.7 = (bf16[240,1280]{1,0:T(8,128)(2,1)}, bf16[240,1280]{1,0:T(8,128)(2,1)S(1)}, u32[]{:S(2)}, u32[]{:S(2)}) collective-permute-start(bf16[240,1280]{1,0:T(8,128)(2,1)} %get-tuple-element.94), channel_id=1, source_target_pairs={{1,0},{2,1},{3,2},{0,3},{5,4},{6,5},{7,6},{4,7},{9,8},{10,9},{11,1... | collective-permute-start | bytes 1843208 | tf_op jit(solution)/shard_map/ppermute | solution.py:337
  71.6 48.6 %collective-permute-start.8 = (bf16[240,1280]{1,0:T(8,128)(2,1)}, bf16[240,1280]{1,0:T(8,128)(2,1)}, u32[]{:S(2)}, u32[]{:S(2)}) collective-permute-start(bf16[240,1280]{1,0:T(8,128)(2,1)} %get-tuple-element.93), channel_id=1, source_target_pairs={{2,0},{3,1},{0,2},{1,3},{6,4},{7,5},{4,6},{5,7},{10,8},{11,9},{8,1... | collective-permute-start | bytes 1843208 | tf_op jit(solution)/shard_map/ppermute | solution.py:337
  71.6 48.6 %collective-permute-start.9 = (bf16[240,1280]{1,0:T(8,128)(2,1)}, bf16[240,1280]{1,0:T(8,128)(2,1)}, u32[]{:S(2)}, u32[]{:S(2)}) collective-permute-start(bf16[240,1280]{1,0:T(8,128)(2,1)} %get-tuple-element.92), channel_id=1, source_target_pairs={{3,0},{0,1},{1,2},{2,3},{7,4},{4,5},{5,6},{6,7},{11,8},{8,9},{9,10... | collective-permute-start | bytes 1843208 | tf_op jit(solution)/shard_map/ppermute | solution.py:337
  72.2 34.9 %collective-permute-start.5 = (bf16[128,960]{1,0:T(8,128)(2,1)S(1)}, bf16[128,960]{1,0:T(8,128)(2,1)S(1)}, u32[]{:S(2)}, u32[]{:S(2)}) collective-permute-start(bf16[128,960]{1,0:T(8,128)(2,1)S(1)} %bitcast.71), channel_id=1, source_target_pairs={{2,0},{3,1},{0,2},{1,3},{6,4},{7,5},{4,6},{5,7},{10,8},{11,9},{8,1... | collective-permute-start | bytes 737288 | tf_op jit(solution)/shard_map/ppermute | solution.py:337
  74.6 34.7 %collective-permute-start.4 = (bf16[128,960]{1,0:T(8,128)(2,1)S(1)}, bf16[128,960]{1,0:T(8,128)(2,1)}, u32[]{:S(2)}, u32[]{:S(2)}) collective-permute-start(bf16[128,960]{1,0:T(8,128)(2,1)S(1)} %bitcast.72), channel_id=1, source_target_pairs={{1,0},{2,1},{3,2},{0,3},{5,4},{6,5},{7,6},{4,7},{9,8},{10,9},{11,1... | collective-permute-start | bytes 737288 | tf_op jit(solution)/shard_map/ppermute | solution.py:337
  90.3 21.1 %all-to-all-start.2 = ((bf16[16,64,128]{2,1,0:T(8,128)(2,1)}), bf16[16,64,128]{2,1,0:T(8,128)(2,1)S(1)}, u32[]{:S(2)}, u32[]{:S(2)}) async-start(bf16[16,64,128]{2,1,0:T(8,128)(2,1)} %get-tuple-element.36), calls=%async_computation.2 | async-start | bytes 524288 | tf_op jit(solution)/shard_map/all_to_all | solution.py:413
  111.5 0.7 copy-start.7
  115.3 10.2 %collective-permute-start.3 = (bf16[128,960]{1,0:T(8,128)(2,1)}, bf16[128,960]{1,0:T(8,128)(2,1)S(1)}, u32[]{:S(2)}, u32[]{:S(2)}) collective-permute-start(bf16[128,960]{1,0:T(8,128)(2,1)} %get-tuple-element.39), channel_id=1, source_target_pairs={{3,0},{0,1},{1,2},{2,3},{7,4},{4,5},{5,6},{6,7},{11,8},{8,9},{9,10... | collective-permute-start | bytes 737288 | tf_op jit(solution)/shard_map/ppermute | solution.py:337
  115.3 15.8 %collective-permute-start.2 = (bf16[128,960]{1,0:T(8,128)(2,1)}, bf16[128,960]{1,0:T(8,128)(2,1)S(1)}, u32[]{:S(2)}, u32[]{:S(2)}) collective-permute-start(bf16[128,960]{1,0:T(8,128)(2,1)} %get-tuple-element.39), channel_id=1, source_target_pairs={{2,0},{3,1},{0,2},{1,3},{6,4},{7,5},{4,6},{5,7},{10,8},{11,9},{8,1... | collective-permute-start | bytes 737288 | tf_op jit(solution)/shard_map/ppermute | solution.py:337
  120.0 11.2 %collective-permute-start.1 = (bf16[128,960]{1,0:T(8,128)(2,1)}, bf16[128,960]{1,0:T(8,128)(2,1)S(1)}, u32[]{:S(2)}, u32[]{:S(2)}) collective-permute-start(bf16[128,960]{1,0:T(8,128)(2,1)} %get-tuple-element.39), channel_id=1, source_target_pairs={{1,0},{2,1},{3,2},{0,3},{5,4},{6,5},{7,6},{4,7},{9,8},{10,9},{11,1... | collective-permute-start | bytes 737288 | tf_op jit(solution)/shard_map/ppermute | solution.py:337
  120.2 11.0 %copy-start.14 = (bf16[128,960]{1,0:T(8,128)(2,1)S(1)}, bf16[128,960]{1,0:T(8,128)(2,1)}, u32[]{:S(2)}) copy-start(bf16[128,960]{1,0:T(8,128)(2,1)} %get-tuple-element.39) | copy-start | bytes 737284
  145.3 30.7 %copy-start.9 = (bf16[64,2048]{1,0:T(8,128)(2,1)S(1)}, bf16[64,2048]{1,0:T(8,128)(2,1)}, u32[]{:S(2)}) copy-start(bf16[64,2048]{1,0:T(8,128)(2,1)} %get-tuple-element.43.qt_ref) | copy-start | bytes 786436
  145.3 8.1 %collective-permute-start.13 = (bf16[128,960]{1,0:T(8,128)(2,1)S(1)}, bf16[128,960]{1,0:T(8,128)(2,1)S(1)}, u32[]{:S(2)}, u32[]{:S(2)}) collective-permute-start(bf16[128,960]{1,0:T(8,128)(2,1)S(1)} %get-tuple-element.100), channel_id=1, source_target_pairs={{3,0},{0,1},{1,2},{2,3},{7,4},{4,5},{5,6},{6,7},{11,8},{8,9},{9,10... | collective-permute-start | bytes 737288 | tf_op jit(solution)/shard_map/ppermute | solution.py:337
  146.9 14.2 %collective-permute-start.14 = (bf16[128,960]{1,0:T(8,128)(2,1)S(1)}, bf16[128,960]{1,0:T(8,128)(2,1)S(1)}, u32[]{:S(2)}, u32[]{:S(2)}) collective-permute-start(bf16[128,960]{1,0:T(8,128)(2,1)S(1)} %get-tuple-element.99), channel_id=1, source_target_pairs={{2,0},{3,1},{0,2},{1,3},{6,4},{7,5},{4,6},{5,7},{10,8},{11,9},{8,1... | collective-permute-start | bytes 737288 | tf_op jit(solution)/shard_map/ppermute | solution.py:337
  149.6 11.5 %collective-permute-start.15 = (bf16[128,960]{1,0:T(8,128)(2,1)S(1)}, bf16[128,960]{1,0:T(8,128)(2,1)S(1)}, u32[]{:S(2)}, u32[]{:S(2)}) collective-permute-start(bf16[128,960]{1,0:T(8,128)(2,1)S(1)} %get-tuple-element.98), channel_id=1, source_target_pairs={{1,0},{2,1},{3,2},{0,3},{5,4},{6,5},{7,6},{4,7},{9,8},{10,9},{11,1... | collective-permute-start | bytes 737288 | tf_op jit(solution)/shard_map/ppermute | solution.py:337
  153.4 7.8 %copy-start.15 = (bf16[128,960]{1,0:T(8,128)(2,1)}, bf16[128,960]{1,0:T(8,128)(2,1)S(1)}, u32[]{:S(2)}) copy-start(bf16[128,960]{1,0:T(8,128)(2,1)S(1)} %collective-permute-done.13.db1) | copy-start | bytes 737284
  161.2 0.7 copy-start.16
  161.2 0.8 copy-start.17
  162.0 15.0 %copy-start.10 = (bf16[64,2048]{1,0:T(8,128)(2,1)S(1)}, bf16[64,2048]{1,0:T(8,128)(2,1)}, u32[]{:S(2)}) copy-start(bf16[64,2048]{1,0:T(8,128)(2,1)} %get-tuple-element.46) | copy-start | bytes 786436
  165.9 16.9 %all-to-all-start.3 = ((bf16[16,64,128]{2,1,0:T(8,128)(2,1)}), bf16[16,64,128]{2,1,0:T(8,128)(2,1)S(1)}, u32[]{:S(2)}, u32[]{:S(2)}) async-start(bf16[16,64,128]{2,1,0:T(8,128)(2,1)} %get-tuple-element.42), calls=%async_computation.3 | async-start | bytes 524288 | tf_op jit(solution)/shard_map/all_to_all | solution.py:448
  182.7 0.7 copy-start.13
  197.0 19.1 %all-to-all-start.4 = ((bf16[16,192,128]{2,1,0:T(8,128)(2,1)}), bf16[16,192,128]{2,1,0:T(8,128)(2,1)S(1)}, u32[]{:S(2)}, u32[]{:S(2)}) async-start(bf16[16,192,128]{2,1,0:T(8,128)(2,1)} %shard_map.174), calls=%async_computation.4 | async-start | bytes 1572864 | tf_op jit(solution)/shard_map/all_to_all | solution.py:492
  216.1 0.9 copy-start
  217.0 33.0 %all-to-all-start.8 = ((bf16[4,240,1280]{2,1,0:T(8,128)(2,1)}), bf16[4,240,1280]{2,1,0:T(8,128)(2,1)S(1)}, u32[]{:S(2)}, u32[]{:S(2)}) async-start(bf16[4,240,1280]{2,1,0:T(8,128)(2,1)} %bitcast.69), calls=%async_computation.8 | async-start | bytes 4915200 | tf_op jit(solution)/shard_map/all_to_all | solution.py:481
  250.0 7.0 %copy-start.19 = (bf16[960,128]{1,0:T(8,128)(2,1)S(1)}, bf16[960,128]{1,0:T(8,128)(2,1)}, u32[]{:S(2)}) copy-start(bf16[960,128]{1,0:T(8,128)(2,1)} %get-tuple-element.54) | copy-start | bytes 737284
  252.4 33.0 %copy-start.11 = (bf16[128,960]{1,0:T(8,128)(2,1)S(1)}, bf16[128,960]{1,0:T(8,128)(2,1)}, u32[]{:S(2)}) copy-start(bf16[128,960]{1,0:T(8,128)(2,1)} %get-tuple-element.55) | copy-start | bytes 737284
  252.4 70.1 %all-to-all-start.5 = ((bf16[4,1616,128]{2,1,0:T(8,128)(2,1)}), bf16[4,1616,128]{2,1,0:T(8,128)(2,1)}, u32[]{:S(2)}, u32[]{:S(2)}) async-start(bf16[4,1616,128]{2,1,0:T(8,128)(2,1)} %broadcast_in_dim.61), calls=%async_computation.5 | async-start | bytes 3309568 | tf_op jit(solution)/shard_map/all_to_all | solution.py:341
  256.9 180.9 %all-reduce.3.cloned.1.call-start = ((), (), s32[]{:S(2)}) async-start(), calls=%async_computation.10 | async-start | bytes 8519680 | tf_op jit(solution)/shard_map/psum | solution.py:489
  310.0 0.9 copy-start.18
  326.1 36.3 %copy-start.6 = (bf16[4,128,960]{2,1,0:T(8,128)(2,1)S(1)}, bf16[4,128,960]{2,1,0:T(8,128)(2,1)}, u32[]{:S(2)}) copy-start(bf16[4,128,960]{2,1,0:T(8,128)(2,1)} %get-tuple-element.40) | copy-start | bytes 2949124
  357.5 22.6 %copy-start.3 = (f32[128,960]{1,0:T(8,128)S(1)}, f32[128,960]{1,0:T(8,128)}, u32[]{:S(2)}) copy-start(f32[128,960]{1,0:T(8,128)} %get-tuple-element.38.h_ref) | copy-start | bytes 1474564
  358.6 23.6 %copy-start.8 = (f32[128,960]{1,0:T(8,128)S(1)}, f32[128,960]{1,0:T(8,128)}, u32[]{:S(2)}) copy-start(f32[128,960]{1,0:T(8,128)} %get-tuple-element.51) | copy-start | bytes 1474564
  358.6 87.8 %all-to-all-start.7 = ((bf16[32,8,1664]{2,1,0:T(8,128)(2,1)}), bf16[32,8,1664]{2,1,0:T(8,128)(2,1)S(1)}, u32[]{:S(2)}, u32[]{:S(2)}) async-start(bf16[32,8,1664]{2,1,0:T(8,128)(2,1)} %broadcast_in_dim.62), calls=%async_computation.7 | async-start | bytes 1703936 | tf_op jit(solution)/shard_map/all_to_all | solution.py:341
  363.3 7.9 %collective-permute-start.12 = (bf16[128,960]{1,0:T(8,128)(2,1)}, bf16[128,960]{1,0:T(8,128)(2,1)S(1)}, u32[]{:S(2)}, u32[]{:S(2)}) collective-permute-start(bf16[128,960]{1,0:T(8,128)(2,1)} %get-tuple-element.103), channel_id=1, source_target_pairs={{1,0},{2,1},{3,2},{0,3},{5,4},{6,5},{7,6},{4,7},{9,8},{10,9},{11,1... | collective-permute-start | bytes 737288 | tf_op jit(solution)/shard_map/ppermute | solution.py:337
  364.4 9.1 %collective-permute-start.11 = (bf16[128,960]{1,0:T(8,128)(2,1)}, bf16[128,960]{1,0:T(8,128)(2,1)S(1)}, u32[]{:S(2)}, u32[]{:S(2)}) collective-permute-start(bf16[128,960]{1,0:T(8,128)(2,1)} %get-tuple-element.104), channel_id=1, source_target_pairs={{2,0},{3,1},{0,2},{1,3},{6,4},{7,5},{4,6},{5,7},{10,8},{11,9},{8,1... | collective-permute-start | bytes 737288 | tf_op jit(solution)/shard_map/ppermute | solution.py:337
  365.2 14.9 %collective-permute-start.10 = (bf16[128,960]{1,0:T(8,128)(2,1)}, bf16[128,960]{1,0:T(8,128)(2,1)}, u32[]{:S(2)}, u32[]{:S(2)}) collective-permute-start(bf16[128,960]{1,0:T(8,128)(2,1)} %get-tuple-element.102), channel_id=1, source_target_pairs={{3,0},{0,1},{1,2},{2,3},{7,4},{4,5},{5,6},{6,7},{11,8},{8,9},{9,10... | collective-permute-start | bytes 737288 | tf_op jit(solution)/shard_map/ppermute | solution.py:337
  373.5 0.7 copy-start.12
  439.9 4.6 %copy-start.4 = (bf16[640,960]{1,0:T(8,128)(2,1)S(1)}, bf16[640,960]{1,0:T(8,128)(2,1)}, u32[]{:S(2)}) copy-start(bf16[640,960]{1,0:T(8,128)(2,1)} %get-tuple-element.87) | copy-start | bytes 3686404
Sparse Core Ops, SparseCore 0:
  37.8 29.6 all-gather.4
  310.2 127.6 all-reduce.2
